TPU v7x, 128 devices: a whole 4x4x4 slice. The times are simulated.
128 devices in a mesh: wide: 16 (over y, x), narrow: 8 (over z, core).
Axes of the slice: x: 4, y: 4, z: 4, core: 2. Of those that a mesh axis runs over, the one named last changes fastest.
Arguments:
- plume_field: bfloat16 [20, 512, 256, 256], P(None, 'wide', 'narrow'), may hold values from -6 to 6
- spectral_weight: float32 [16, 16, 16, 800], P('wide', 'narrow'), may hold values from -0.015625 to 0.015625
- linear_weight: bfloat16 [20, 20], replicated, may hold values from -1.25 to 1.25
- channel_bias: float32 [20], replicated, may hold values from -3 to 3
Outputs:
- layer_out: bfloat16 [20, 512, 256, 256], P(None, 'wide', 'narrow')
All inputs are finite; a program needn't handle non-finite values.
Results may differ from a plain program's by a relative error of at most 0.0053.
Values may be sent and summed in bfloat16 or wider, within the bound.
A program may use at most 128 MiB of HBM per device.

v0:
```python
import functools
import math

import jax
import jax.numpy as jnp
import ml_dtypes
import numpy as np
from jax import lax
from jax.experimental import pallas as pl
from jax.experimental.pallas import tpu as pltpu
from jax.sharding import PartitionSpec as P

MESH = pl.DeviceIdType.MESH
C, NX, NY, NZ, K = 20, 256, 512, 256, 16
YL, ZL = 32, 32
CELLS = YL * ZL
LANES = 2 * K * C
BF16, F32 = jnp.bfloat16, jnp.float32
GROUPS = ((0, 8, 0), (8, 8, 256), (16, 4, 512))
VMEM_LIMIT = 56 * 2**20


def np_bf16(a):
    return np.asarray(a, np.float32).astype(ml_dtypes.bfloat16)


def signed(m):
    return np.where(m < K // 2, m, m - K)


def x_tables():
    places, orders = np.arange(NX), np.arange(K)
    angles = np.mod(places[:, None] * orders[None, :], NX).astype(np.float32) * np.float32(2.0 * math.pi / NX)
    cos_tab, sin_tab = np.cos(angles), np.sin(angles)
    doubled = np.where(orders == 0, 1.0, 2.0).astype(np.float32)
    forward = np_bf16(np.stack([cos_tab, -sin_tab], -1))
    inverse = np_bf16(np.stack([cos_tab * doubled, -sin_tab * doubled], -1))
    return forward, inverse


def forward_table():
    forward = x_tables()[0].reshape(NX, 2 * K)
    wide = np.zeros((8, NX, 2 * K, 8), ml_dtypes.bfloat16)
    slim = np.zeros((4, NX, 2 * K, 4), ml_dtypes.bfloat16)
    for c in range(8):
        wide[c, :, :, c] = forward
    for c in range(4):
        slim[c, :, :, c] = forward
    return wide.reshape(8 * NX, 256), slim.reshape(4 * NX, 128)


def inverse_table():
    inverse = x_tables()[1].reshape(NX, 2 * K).T
    return np.repeat(inverse, 4, axis=0)


def cell_angles():
    f = signed(np.arange(K))
    y = np.mod(f[:, None] * np.arange(YL)[None, :], NY) / NY
    z = np.mod(f[:, None] * np.arange(ZL)[None, :], NZ) / NZ
    turns = y[:, None, :, None] + z[None, :, None, :]
    return 2.0 * math.pi * turns.reshape(K * K, CELLS)


def analysis_table():
    angles = cell_angles()
    return np_bf16(np.concatenate([np.cos(angles), np.sin(angles)], 0))


def synthesis_table():
    angles = cell_angles().T
    return np_bf16(np.concatenate([np.cos(angles), np.sin(angles)], 1))


def offset_phase(wide, narrow, rows):
    row = lax.broadcasted_iota(jnp.int32, (rows, 128), 0)
    j, l = row // K, row % K
    fj = jnp.where(j < K // 2, j, j - K)
    fl = jnp.where(l < K // 2, l, l - K)
    step = (fj * wide + 2 * fl * narrow) & 15
    cos_v = jnp.zeros((rows, 128), F32)
    sin_v = jnp.zeros((rows, 128), F32)
    for k in range(16):
        c, s = math.cos(math.pi * k / 8), math.sin(math.pi * k / 8)
        cos_v = jnp.where(step == k, F32(c), cos_v)
        sin_v = jnp.where(step == k, F32(s), sin_v)
    return cos_v, sin_v


def swap_pair(v, half):
    lanes = v.shape[1]
    lane = lax.broadcasted_iota(jnp.int32, v.shape, 1)
    return jnp.where((lane // half) % 2 == 0, pltpu.roll(v, lanes - half, 1), pltpu.roll(v, half, 1))


def lane_sign(shape, half):
    lane = lax.broadcasted_iota(jnp.int32, shape, 1)
    return jnp.where((lane // half) % 2 == 0, F32(1.0), F32(-1.0))


def row_of(pair, c):
    if c < 8:
        return pair * 8 + c
    if c < 16:
        return 16 + pair * 8 + c - 8
    return 32 + pair * 4 + c - 16


def spectra_kernel(
    n_wide, n_narrow,
    plume, w_ref, ta_ref, tb_ref, e_ref, m_ref,
    x_buf, a_buf, s_send, s_recv, t_send, t_recv, q_buf, wt_buf, m_send, m_recv, g_send, g_recv, phase,
    in_sem, s_ss, s_rs, t_ss, t_rs, m_ss, m_rs, g_ss, g_rs,
):
    wide, narrow = lax.axis_index("wide"), lax.axis_index("narrow")
    loads = []
    for g, (c0, nc, _) in enumerate(GROUPS):
        copy = pltpu.make_async_copy(plume.at[pl.ds(c0, nc)], x_buf.at[pl.ds(c0, nc)], in_sem.at[g])
        copy.start()
        loads.append(copy)

    barrier = pltpu.get_barrier_semaphore()

    def greet_narrow(i, _):
        pl.semaphore_signal(barrier, inc=1, device_id=(wide, lax.rem(narrow + i, n_narrow)), device_id_type=MESH)
        return 0

    def greet_wide(i, _):
        pl.semaphore_signal(barrier, inc=1, device_id=(lax.rem(wide + i, n_wide), narrow), device_id_type=MESH)
        return 0

    lax.fori_loop(1, n_narrow, greet_narrow, 0)
    lax.fori_loop(1, n_wide, greet_wide, 0)

    cos_v, sin_v = offset_phase(wide, narrow, K * K)
    phase[0] = cos_v
    phase[1] = sin_v
    for k in range(7):
        width = min(128, 2 * C * C - 128 * k)
        wt_buf[pl.ds(128 * k, width), :] = w_ref[:, pl.ds(128 * k, width)].T
    scale = F32(1.0 / math.sqrt(NX * NY * NZ))

    def s_copy(g, i):
        _, nc, lane0 = GROUPS[g]
        to = lax.rem(narrow + i, n_narrow)
        lanes = pl.ds(lane0, 32 * nc)
        return pltpu.make_async_remote_copy(
            src_ref=s_send.at[to, :, lanes], dst_ref=s_recv.at[i, :, lanes],
            send_sem=s_ss.at[g, i], recv_sem=s_rs.at[g, i],
            device_id=(wide, to), device_id_type=MESH)

    for g, (c0, nc, lane0) in enumerate(GROUPS):
        loads[g].wait()
        table = ta_ref if nc == 8 else tb_ref
        width = 32 * nc
        for r in range(4):
            rows = jnp.concatenate(
                [x_buf[c, pl.ds(8 * r, 8)].reshape(256, NX) for c in range(c0, c0 + nc)], axis=1)
            a_buf[pl.ds(256 * r, 256), pl.ds(0, width)] = jnp.dot(
                rows, table[...], preferred_element_type=F32).astype(BF16)
        a = a_buf[:, pl.ds(0, width)]
        half = nc
        for h in range(2):
            rows = pl.ds(128 * h, 128)
            g_cos = jnp.dot(e_ref[rows, :], a, preferred_element_type=F32)
            g_sin = jnp.dot(e_ref[pl.ds(256 + 128 * h, 128), :], a, preferred_element_type=F32)
            for part in range(width // 128):
                lanes = slice(128 * part, 128 * part + 128)
                gc, gs = g_cos[:, lanes], g_sin[:, lanes]
                pc, ps = phase[0, rows] * scale, phase[1, rows] * scale
                rc = pc * gc - ps * gs
                rs = ps * gc + pc * gs
                s = rc + lane_sign((128, 128), half) * swap_pair(rs, half)
                s_send[pl.ds(4 * h, 4), :, pl.ds(lane0 + 128 * part, 128)] = s.astype(BF16).reshape(4, 32, 128)
        if g == 0:
            pl.semaphore_wait(barrier, n_narrow + n_wide - 2)

        def send(i, _, g=g):
            s_copy(g, i).start()
            return 0

        lax.fori_loop(1, n_narrow, send, 0)

    s_recv[0] = s_send[narrow]
    for g in range(len(GROUPS)):
        def arrive(i, _, g=g):
            s_copy(g, i).wait_recv()
            return 0

        lax.fori_loop(1, n_narrow, arrive, 0)
    total = s_recv[0].astype(F32)
    for i in range(1, n_narrow):
        total = total + s_recv[i].astype(F32)

    for k in range(K):
        pieces = [total[:, 16 * k:16 * k + 16], total[:, 256 + 16 * k:256 + 16 * k + 16],
                  total[:, 512 + 8 * k:512 + 8 * k + 8]]
        row = jnp.concatenate(pieces, axis=1)
        pad = jnp.zeros((16, 24), F32)
        t_send[k] = jnp.concatenate([row[:16], pad, row[16:], pad], axis=1).astype(BF16)

    def t_copy(i):
        to = lax.rem(wide + i, n_wide)
        return pltpu.make_async_remote_copy(
            src_ref=t_send.at[to], dst_ref=t_recv.at[i], send_sem=t_ss.at[i], recv_sem=t_rs.at[i],
            device_id=(to, narrow), device_id_type=MESH)

    def t_start(i, _):
        t_copy(i).start()
        return 0

    def t_arrive(i, _):
        t_copy(i).wait_recv()
        return 0

    lax.fori_loop(1, n_wide, t_start, 0)
    t_recv[0] = t_send[wide]
    lax.fori_loop(1, n_wide, t_arrive, 0)
    total = t_recv[0].astype(F32)
    for i in range(1, n_wide):
        total = total + t_recv[i].astype(F32)
    turned = total.T
    q_buf[...] = jnp.concatenate([turned[0:64], turned[64:128]], axis=1)

    out_re = jnp.zeros((C, 32), F32)
    out_im = jnp.zeros((C, 32), F32)
    for c in range(C):
        s_re = q_buf[pl.ds(row_of(0, c), 1), :]
        s_im = q_buf[pl.ds(row_of(1, c), 1), :]
        w_re = wt_buf[pl.ds(C * c, C), :]
        w_im = wt_buf[pl.ds(C * C + C * c, C), :]
        out_re = out_re + (w_re * s_re - w_im * s_im)
        out_im = out_im + (w_re * s_im + w_im * s_re)
    rows = []
    for j in range(5):
        rows += [out_re[4 * j:4 * j + 4], out_im[4 * j:4 * j + 4]]
    rows.append(jnp.zeros((24, 32), F32))
    rows = jnp.concatenate(rows, axis=0)
    rows = jnp.concatenate([rows[:, :16], rows[:, 16:]], axis=0)
    m_send[...] = rows.T.astype(BF16)

    def m_copy(i):
        to = lax.rem(wide + i, n_wide)
        return pltpu.make_async_remote_copy(
            src_ref=m_send, dst_ref=m_recv.at[wide], send_sem=m_ss.at[i], recv_sem=m_rs.at[i],
            device_id=(to, narrow), device_id_type=MESH)

    def m_start(i, _):
        m_copy(i).start()
        return 0

    def m_arrive(i, _):
        m_copy(i).wait_recv()
        return 0

    lax.fori_loop(1, n_wide, m_start, 0)
    m_recv[wide] = m_send[...]
    lax.fori_loop(1, n_wide, m_arrive, 0)
    tiles = [m_recv[k].astype(F32) for k in range(K)]
    for j2 in range(2):
        for j in range(5):
            at = 64 * j2 + 8 * j
            lanes = jnp.concatenate([tiles[k][:, at:at + 8] for k in range(K)], axis=1)
            g_send[pl.ds(16 * j2, 16), pl.ds(128 * j, 128)] = lanes.astype(BF16)

    def g_copy(i):
        to = lax.rem(narrow + i, n_narrow)
        return pltpu.make_async_remote_copy(
            src_ref=g_send, dst_ref=g_recv.at[narrow], send_sem=g_ss.at[i], recv_sem=g_rs.at[i],
            device_id=(wide, to), device_id_type=MESH)

    def g_start(i, _):
        g_copy(i).start()
        return 0

    def g_arrive(i, _):
        g_copy(i).wait_recv()
        return 0

    lax.fori_loop(1, n_narrow, g_start, 0)
    g_recv[narrow] = g_send[...]
    lax.fori_loop(1, n_narrow, g_arrive, 0)

    for j in range(n_narrow):
        pc, ps = phase[0, pl.ds(32 * j, 32)], phase[1, pl.ds(32 * j, 32)]
        for part in range(5):
            v = g_recv[j, :, pl.ds(128 * part, 128)].astype(F32)
            sw = -lane_sign((32, 128), 4) * swap_pair(v, 4)
            m_ref[pl.ds(32 * j, 32), pl.ds(128 * part, 128)] = (pc * v + ps * sw).astype(BF16)
            m_ref[pl.ds(256 + 32 * j, 32), pl.ds(128 * part, 128)] = (pc * sw - ps * v).astype(BF16)

    def drain_narrow(i, _):
        for g in range(len(GROUPS)):
            s_copy(g, i).wait_send()
        g_copy(i).wait_send()
        return 0

    def drain_wide(i, _):
        t_copy(i).wait_send()
        m_copy(i).wait_send()
        return 0

    lax.fori_loop(1, n_narrow, drain_narrow, 0)
    lax.fori_loop(1, n_wide, drain_wide, 0)


def spectra(n_wide, n_narrow, plume, weight, ta, tb, e):
    vmem = pl.BlockSpec(memory_space=pltpu.VMEM)
    dma = pltpu.SemaphoreType.DMA
    return pl.pallas_call(
        functools.partial(spectra_kernel, n_wide, n_narrow),
        out_shape=jax.ShapeDtypeStruct((2 * K * K, LANES), BF16),
        in_specs=[pl.BlockSpec(memory_space=pl.ANY)] + [vmem] * 4,
        out_specs=vmem,
        scratch_shapes=[
            pltpu.VMEM((C, YL, ZL, NX), BF16),
            pltpu.VMEM((CELLS, 256), BF16),
            pltpu.VMEM((n_narrow, 32, LANES), BF16),
            pltpu.VMEM((n_narrow, 32, LANES), BF16),
            pltpu.VMEM((K, 16, 128), BF16),
            pltpu.VMEM((n_wide, 16, 128), BF16),
            pltpu.VMEM((64, 32), F32),
            pltpu.VMEM((2 * C * C, 32), F32),
            pltpu.VMEM((16, 128), BF16),
            pltpu.VMEM((n_wide, 16, 128), BF16),
            pltpu.VMEM((32, LANES), BF16),
            pltpu.VMEM((n_narrow, 32, LANES), BF16),
            pltpu.VMEM((2, K * K, 128), F32),
            dma((3,)),
            dma((3, n_narrow)), dma((3, n_narrow)),
            dma((n_wide,)), dma((n_wide,)),
            dma((n_wide,)), dma((n_wide,)),
            dma((n_narrow,)), dma((n_narrow,)),
        ],
        compiler_params=pltpu.CompilerParams(
            collective_id=0, has_side_effects=True, vmem_limit_bytes=VMEM_LIMIT),
        name="spectra",
    )(plume, weight, ta, tb, e)


CHUNKS = 4


def output_kernel(plume, m_ref, e_ref, lw_ref, bias_ref, xi_ref, out, x_buf, o_buf, b_buf, kron, rhs, in_sem, out_sem):
    yt = YL // CHUNKS

    def load(i):
        rows = pl.ds(i * yt, yt)
        return pltpu.make_async_copy(plume.at[:, rows], x_buf.at[:, rows], in_sem.at[i])

    def store(i):
        rows = pl.ds(i * yt, yt)
        return pltpu.make_async_copy(o_buf.at[:, rows], out.at[:, rows], out_sem.at[i])

    for i in range(CHUNKS):
        load(i).start()
    spread = jnp.where(
        lax.broadcasted_iota(jnp.int32, (320, C), 0) // 16 == lax.broadcasted_iota(jnp.int32, (320, C), 1),
        F32(1.0), F32(0.0)).astype(BF16)
    rows20 = jnp.dot(spread, lw_ref[...], preferred_element_type=F32).astype(BF16)
    across = jnp.where(
        lax.broadcasted_iota(jnp.int32, (C, 384), 1) // 16 == lax.broadcasted_iota(jnp.int32, (C, 384), 0),
        F32(1.0), F32(0.0)).astype(BF16)
    full = jnp.dot(rows20, across, preferred_element_type=F32)
    row = lax.broadcasted_iota(jnp.int32, (320, 384), 0)
    col = lax.broadcasted_iota(jnp.int32, (320, 384), 1)
    full = jnp.where((row % 16) == (col % 16), full, F32(0.0))
    bias = bias_ref[...]
    b1 = bias.astype(BF16).astype(F32)
    b2 = (bias - b1).astype(BF16).astype(F32)
    b3 = bias - b1 - b2
    full = jnp.where(col == 320, b1, full)
    full = jnp.where(col == 321, b2, full)
    full = jnp.where(col == 322, b3, full)
    kron[...] = full.astype(BF16)
    for s in range(2):
        rhs[s, pl.ds(0, 128), :] = xi_ref[...]
        rhs[s, pl.ds(192, 64), :] = jnp.where(
            lax.broadcasted_iota(jnp.int32, (64, NX), 0) < 16, F32(1.0), F32(0.0)).astype(BF16)
    lane = lax.broadcasted_iota(jnp.int32, (16, 128), 1) % 4
    masks = [lane == k for k in range(4)]

    def chunk(i, _):
        load(i).wait()
        cells = yt * ZL
        b_buf[...] = jnp.dot(
            e_ref[pl.ds(pl.multiple_of(i * cells, cells), cells), :], m_ref[...],
            preferred_element_type=F32).astype(BF16)
        for q in range(cells // 16):
            y, z, s = i * yt + q // 2, (q % 2) * 16, q % 2
            xs = x_buf[:, y, pl.ds(z, 16), :].reshape(320, NX)
            rhs[s, pl.ds(128, 64), :] = xs[256:]
            parts = []
            for o in range(C):
                v = b_buf[pl.ds(16 * q, 16), pl.ds(128 * (o // 4), 128)]
                parts.append(jnp.where(masks[o % 4], v, jnp.zeros_like(v)))
            left = jnp.concatenate([jnp.concatenate(parts, 0), kron[:, pl.ds(256, 128)]], 1)
            acc = jnp.dot(kron[:, pl.ds(0, 256)], xs[:256], preferred_element_type=F32)
            acc = acc + jnp.dot(left, rhs[s], preferred_element_type=F32)
            half = 0.5 * acc
            y_out = half + half * lax.erf(acc * F32(math.sqrt(0.5)))
            o_buf[:, y, pl.ds(z, 16), :] = y_out.astype(BF16).reshape(C, 16, NX)
        store(i).start()
        return 0

    lax.fori_loop(0, CHUNKS, chunk, 0)
    for i in range(CHUNKS):
        store(i).wait()


def output(plume, m, e, lw, bias, xi):
    vmem = pl.BlockSpec(memory_space=pltpu.VMEM)
    anywhere = pl.BlockSpec(memory_space=pl.ANY)
    dma = pltpu.SemaphoreType.DMA
    return pl.pallas_call(
        output_kernel,
        out_shape=jax.ShapeDtypeStruct((C, YL, ZL, NX), BF16),
        in_specs=[anywhere] + [vmem] * 5,
        out_specs=anywhere,
        scratch_shapes=[
            pltpu.VMEM((C, YL, ZL, NX), BF16),
            pltpu.VMEM((C, YL, ZL, NX), BF16),
            pltpu.VMEM((CELLS // CHUNKS, LANES), BF16),
            pltpu.VMEM((320, 384), BF16),
            pltpu.VMEM((2, 256, NX), BF16),
            dma((CHUNKS,)), dma((CHUNKS,)),
        ],
        compiler_params=pltpu.CompilerParams(vmem_limit_bytes=VMEM_LIMIT),
        name="output",
    )(plume, m, e, lw, bias, xi)


def on_device(n_wide, n_narrow, plume, weight, linear_weight, channel_bias):
    ta, tb = forward_table()
    m = spectra(
        n_wide, n_narrow, plume, weight.reshape(32, 2 * C * C),
        jnp.asarray(ta), jnp.asarray(tb), jnp.asarray(analysis_table()))
    bias = jnp.repeat(channel_bias, 16)[:, None]
    return output(
        plume, m, jnp.asarray(synthesis_table()), linear_weight, bias, jnp.asarray(inverse_table()))


def solution(mesh):
    n_wide, n_narrow = mesh.shape["wide"], mesh.shape["narrow"]
    return jax.shard_map(
        functools.partial(on_device, n_wide, n_narrow), mesh=mesh,
        in_specs=(P(None, "wide", "narrow", None), P("wide", "narrow", None, None), P(), P()),
        out_specs=P(None, "wide", "narrow", None), check_vma=False)
```

profile of v0, /device:TPU:1, one launch (start us, length us, event | category | flops | bytes accessed | tf_op | source)
XLA Modules:
  0.0 48.4 jit_solution(10849640468928203894)
XLA Ops:
  0.0 0.7 %broadcast_in_dim.3 = f32[20,16]{1,0:T(8,128)S(1)} broadcast(f32[20]{0:T(128)} %param.12), dimensions={0} | broadcast | bytes 1360 | tf_op jit(solution)/shard_map/broadcast_in_dim | solution.py:438
  0.7 0.8 %broadcast_in_dim_reshape.4.bias_ref = f32[320,1]{1,0:T(8,128)} reshape(f32[20,16]{1,0:T(8,128)S(1)} %broadcast_in_dim.3) | data formatting | bytes 2560 | tf_op jit(solution)/shard_map/broadcast_in_dim;reshape | solution.py:438
  1.5 34.6 %spectra.1.m_ref = bf16[512,640]{1,0:T(8,128)(2,1)} custom-call(bf16[20,32,32,256]{3,2,1,0:T(8,128)(2,1)} %plume.3, f32[32,800]{1,0:T(8,128)} %bitcast.1, bf16[2048,256]{1,0:T(8,128)(2,1)} %constant.10.clone.ta_ref, bf16[1024,128]{1,0:T(8,128)(2,1)} %constant.11.clone.tb_ref, bf16[512,1024]{1,0:T(8,128)(2,1)} %constant.12.clone.e_ref), custom_call_target="tpu_custom_call" | custom-call | tf_op jit(solution)/shard_map/spectra/pallas_call | solution.py:310
  36.1 12.2 %output.1 = bf16[20,32,32,256]{3,2,1,0:T(8,128)(2,1)} custom-call(bf16[20,32,32,256]{3,2,1,0:T(8,128)(2,1)} %plume.3, bf16[512,640]{1,0:T(8,128)(2,1)} %spectra.1.m_ref, bf16[1024,512]{1,0:T(8,128)(2,1)} %constant.13.clone.e_ref, bf16[20,20]{1,0:T(8,128)(2,1)} %lw_ref.1, f32[320,1]{1,0:T(8,128)} %broadcast_in_dim_reshape.4.bias_ref, ...), custom_call_target="tpu_custom_call" | custom-call | tf_op jit(solution)/shard_map/output/pallas_call | solution.py:415
where the time goes:
time: 48.5 us; the launch traced here: 48.4 us
  Pallas kernels  46.9 us (97%)
  local copies, waits for them, and re-layouts  1.5 us (3%)
    pallas_call x1, Pallas kernels, spectra(): pl.pallas_call(functools.partial(spectra_kernel, n_wide, n_narrow), out_s...  34.6 us
    pallas_call x1, Pallas kernels, output(): pl.pallas_call(output_kernel, out_shape=jax.ShapeDtypeStruct((C, YL, ZL,...  12.2 us

commit v1 on v0

v1 whole, which is shorter than its diff:
```python
import math

import jax
import jax.numpy as jnp
import ml_dtypes
import numpy as np
from jax import lax
from jax.experimental import pallas as pl
from jax.experimental.pallas import tpu as pltpu
from jax.sharding import PartitionSpec as P

MESH = pl.DeviceIdType.MESH
C, NX, NY, NZ, K = 20, 256, 512, 256, 16
YL, ZL = 32, 32
CELLS = YL * ZL
LANES = 2 * K * C
BF16, F32 = jnp.bfloat16, jnp.float32
GROUPS = ((0, 8, 0), (8, 8, 256), (16, 4, 512))
CONTRACT_LANES = (((1,), (1,)), ((), ()))


def np_bf16(a):
    return np.asarray(a, np.float32).astype(ml_dtypes.bfloat16)


def signed(m):
    return np.where(m < K // 2, m, m - K)


def x_tables():
    places, orders = np.arange(NX), np.arange(K)
    angles = np.mod(places[:, None] * orders[None, :], NX).astype(np.float32) * np.float32(2.0 * math.pi / NX)
    cos_tab, sin_tab = np.cos(angles), np.sin(angles)
    doubled = np.where(orders == 0, 1.0, 2.0).astype(np.float32)
    forward = np_bf16(np.stack([cos_tab, -sin_tab], -1))
    inverse = np_bf16(np.stack([cos_tab * doubled, -sin_tab * doubled], -1))
    return forward, inverse


def forward_table():
    forward = x_tables()[0].reshape(NX, 2 * K).T
    return np.repeat(forward, 8, axis=0), np.repeat(forward, 4, axis=0)


def inverse_table():
    inverse = x_tables()[1].reshape(NX, 2 * K).T
    return np.repeat(inverse, 4, axis=0)


def mode_order():
    core, z, j2, l = np.meshgrid(np.arange(2), np.arange(4), np.arange(2), np.arange(K), indexing="ij")
    return (2 * (2 * z + core) + j2).reshape(-1), l.reshape(-1)


def cell_angles():
    j, l = mode_order()
    fj, fl = signed(j), signed(l)
    y = np.mod(fj[:, None] * np.arange(YL)[None, :], NY) / NY
    z = np.mod(fl[:, None] * np.arange(ZL)[None, :], NZ) / NZ
    turns = y[:, :, None] + z[:, None, :]
    return 2.0 * math.pi * turns.reshape(K * K, CELLS)


def mode_table():
    angles = cell_angles().T
    return np_bf16(np.concatenate([np.cos(angles), np.sin(angles)], 1))


def offset_phase(wide, narrow):
    lane = lax.broadcasted_iota(jnp.int32, (8, 256), 1)
    l = lane % 16
    j = 2 * (2 * ((lane // 32) % 4) + lane // 128) + (lane // 16) % 2
    fj = jnp.where(j < K // 2, j, j - K)
    fl = jnp.where(l < K // 2, l, l - K)
    step = (fj * wide + 2 * fl * narrow) & 15
    cos_v = jnp.zeros((8, 256), F32)
    sin_v = jnp.zeros((8, 256), F32)
    for k in range(16):
        c, s = math.cos(math.pi * k / 8), math.sin(math.pi * k / 8)
        cos_v = jnp.where(step == k, F32(c), cos_v)
        sin_v = jnp.where(step == k, F32(s), sin_v)
    return cos_v, sin_v


def row_of(pair, c):
    if c < 8:
        return pair * 8 + c
    if c < 16:
        return 16 + pair * 8 + c - 8
    return 32 + pair * 4 + c - 16


def block_turn(tiles):
    shape = tiles[0].shape
    block = lax.broadcasted_iota(jnp.int32, shape, len(shape) - 1) // 32
    out = []
    for r in range(4):
        v = tiles[r]
        for b in range(4):
            if b != r:
                v = jnp.where(block == b, pltpu.roll(tiles[b], (32 * (b - r)) % 128, len(shape) - 1), v)
        out.append(v)
    return out


def spectra_kernel(
    plume, w_hbm, t8_hbm, t4_hbm, e_ref,
    m_ref,
    x_buf, w_ref, t8_ref, t4_ref, e_buf, tab8, tab4, a_buf, sib_send, sib_recv, mine, s_send, s_recv, q_buf, wt_buf, m_send, m_recv,
    g_buf, phase,
    in_sem, w_sem, e_sem, c_ss, c_rs, s_ss, s_rs, m_ss, m_rs, g_ss, g_rs,
):
    wide, narrow = lax.axis_index("wide"), lax.axis_index("narrow")
    y, x = lax.div(wide, 4), lax.rem(wide, 4)
    z, core = lax.div(narrow, 2), lax.rem(narrow, 2)
    sibling = (wide, narrow + 1 - 2 * core)
    e_copy = pltpu.make_async_copy(e_ref, e_buf, e_sem)
    small = [pltpu.make_async_copy(src, dst, w_sem.at[i]) for i, (src, dst) in enumerate(
        ((t8_hbm, t8_ref), (t4_hbm, t4_ref), (w_hbm, w_ref)))]
    for copy in small:
        copy.start()
    loads = []
    for g, (c0, nc, _) in enumerate(GROUPS):
        copy = pltpu.make_async_copy(plume.at[pl.ds(c0, nc)], x_buf.at[pl.ds(c0, nc)], in_sem.at[g])
        copy.start()
        loads.append(copy)
        if g == 0:
            e_copy.start()

    rows_of_chips = [4 * lax.rem(y + d, 4) for d in range(4)]
    places = [lax.rem(x + d, 4) for d in range(4)]
    wides = [[r + p for p in places] for r in rows_of_chips]
    layers = [lax.rem(z + d, 4) for d in range(4)]
    narrows = [2 * v + core for v in layers]
    far = (0, 1, 2, 1)
    others = sorted(
        [(16 * dz + 4 * dy + dx, dz, dy, dx) for dz in range(4) for dy in range(4) for dx in range(4)][1:],
        key=lambda v: (-(far[v[1]] + far[v[2]] + far[v[3]]), v))

    barrier = pltpu.get_barrier_semaphore()
    pl.semaphore_signal(barrier, inc=1, device_id=sibling, device_id_type=MESH)

    for _, dz, dy, dx in others:
        pl.semaphore_signal(barrier, inc=1, device_id=(wides[dy][dx], narrows[dz]), device_id_type=MESH)

    for copy in small:
        copy.wait()
    r8 = lax.broadcasted_iota(jnp.int32, (256, NX), 0) % 8
    r4 = lax.broadcasted_iota(jnp.int32, (128, NX), 0) % 4
    for c in range(8):
        tab8[:, pl.ds(NX * c, NX)] = jnp.where(r8 == c, t8_ref[...], jnp.zeros((), BF16))
    for c in range(4):
        tab4[:, pl.ds(NX * c, NX)] = jnp.where(r4 == c, t4_ref[...], jnp.zeros((), BF16))
    cos_v, sin_v = offset_phase(wide, narrow)
    for h in range(2):
        phase[0, h] = cos_v[:, 128 * h:128 * h + 128]
        phase[1, h] = sin_v[:, 128 * h:128 * h + 128]
    scale = F32(1.0 / math.sqrt(NX * NY * NZ))
    pc, ps = cos_v * scale, sin_v * scale
    for k in range(7):
        width = min(128, 2 * C * C - 128 * k)
        wt_buf[pl.ds(128 * k, width), :] = w_ref[:, pl.ds(128 * k, width)].T

    def c_copy(g):
        c0, nc, row0 = GROUPS[g]
        rows = pl.ds(row0, 32 * nc)
        return pltpu.make_async_remote_copy(
            src_ref=sib_send.at[1 - core, rows], dst_ref=sib_recv.at[rows],
            send_sem=c_ss.at[g], recv_sem=c_rs.at[g], device_id=sibling, device_id_type=MESH)

    for g, (c0, nc, row0) in enumerate(GROUPS):
        loads[g].wait()
        table = tab8 if nc == 8 else tab4
        width = 32 * nc
        for r in range(4):
            rows = jnp.concatenate(
                [x_buf[c, pl.ds(8 * r, 8)].reshape(256, NX) for c in range(c0, c0 + nc)], axis=1)
            a_buf[pl.ds(0, width), pl.ds(256 * r, 256)] = lax.dot_general(
                table[...], rows, CONTRACT_LANES, preferred_element_type=F32).astype(BF16)
        if g == 0:
            e_copy.wait()
        turned = jnp.dot(a_buf[pl.ds(0, width), :], e_buf[...], preferred_element_type=F32)
        g_cos = turned[:, :256].reshape(width // 8, 8, 256)
        g_sin = turned[:, 256:].reshape(width // 8, 8, 256)
        rc = pc * g_cos - ps * g_sin
        rs = ps * g_cos + pc * g_sin
        if nc == 8:
            rc, rs = rc.reshape(K, 2, 8, 256), rs.reshape(K, 2, 8, 256)
            s = jnp.stack([rc[:, 0] + rs[:, 1], rc[:, 1] - rs[:, 0]], axis=1)
        else:
            first = lax.broadcasted_iota(jnp.int32, (K, 8, 256), 1) < 4
            turn = pltpu.roll(rs, 4, 1)
            s = rc + jnp.where(first, turn, -turn)
        s = s.reshape(width, 256)
        sib_send[0, pl.ds(row0, width), :] = s[:, :128].astype(BF16)
        sib_send[1, pl.ds(row0, width), :] = s[:, 128:].astype(BF16)
        mine[pl.ds(row0, width), :] = jnp.where(core == 0, s[:, :128], s[:, 128:])
        if g == 0:
            pl.semaphore_wait(barrier, 64)
        c_copy(g).start()

    for g in range(len(GROUPS)):
        c_copy(g).wait_recv()

    def both(g, size):
        _, nc, row0 = GROUPS[g]
        rows = pl.ds(row0, 32 * nc)
        return (mine[rows, :] + sib_recv[rows, :].astype(F32)).reshape(size)

    g0, g1, g2 = both(0, (K, 2, 8, 128)), both(1, (K, 2, 8, 128)), both(2, (K, 8, 128))
    dense = block_turn([g0[:, 0], g0[:, 1], g1[:, 0], g1[:, 1]])
    for r in range(4):
        rest = g2 if r == 0 else pltpu.roll(g2, 128 - 32 * r, 2)
        s_send[r] = jnp.concatenate([dense[r], rest], axis=1).astype(BF16)

    for slot, dz, dy, dx in others:
        pltpu.make_async_remote_copy(
            src_ref=s_send.at[layers[dz], wides[dy][dx]], dst_ref=s_recv.at[slot],
            send_sem=s_ss, recv_sem=s_rs.at[dz],
            device_id=(wides[dy][dx], narrows[dz]), device_id_type=MESH).start()

    def arrived(buf, sems, part):
        ref = buf.at[pl.ds(max(1, 16 * part), 16 if part else 15)]
        pltpu.make_async_copy(ref, ref, sems.at[part]).wait()

    total = s_send[z, wide].astype(F32)
    for part in (0, 1, 3, 2):
        first = max(1, 16 * part)
        arrived(s_recv, s_rs, part)
        total = total + jnp.sum(s_recv[pl.ds(first, 16 * part + 16 - first)].astype(F32), axis=0)
    for t in range(4):
        v = total[0:8] if t == 0 else pltpu.roll(total[0:8], 128 - 32 * t, 1)
        q_buf[pl.ds(8 * t, 8), :] = v[:, :32]
    q_buf[pl.ds(32, 8), :] = total[8:16, :32]

    out_re = jnp.zeros((C, 32), F32)
    out_im = jnp.zeros((C, 32), F32)
    for c in range(C):
        s_re = q_buf[pl.ds(row_of(0, c), 1), :]
        s_im = q_buf[pl.ds(row_of(1, c), 1), :]
        w_re = wt_buf[pl.ds(C * c, C), :]
        w_im = wt_buf[pl.ds(C * C + C * c, C), :]
        out_re = out_re + (w_re * s_re - w_im * s_im)
        out_im = out_im + (w_re * s_im + w_im * s_re)
    tiles = [jnp.concatenate([out_re[4 * j:4 * j + 4], out_im[4 * j:4 * j + 4]], axis=0) for j in range(5)]
    m_send[...] = jnp.concatenate(
        [jnp.concatenate(tiles[:4], axis=1),
         jnp.concatenate([tiles[4], jnp.zeros((8, 96), F32)], axis=1)], axis=0).astype(BF16)

    for slot, dz, dy, dx in others:
        pltpu.make_async_remote_copy(
            src_ref=m_send, dst_ref=m_recv.at[z, wide], send_sem=m_ss, recv_sem=m_rs,
            device_id=(wides[dy][dx], narrows[dz]), device_id_type=MESH).start()
    m_recv[z, wide] = m_send[...]

    def all_but_one(sem):
        ref = s_recv.at[pl.ds(1, 63)]
        pltpu.make_async_copy(ref, ref, sem).wait()

    all_but_one(m_rs)
    got = [m_recv[r].astype(F32) for r in range(4)]
    dense = block_turn([v[:, :8] for v in got])
    block = lax.broadcasted_iota(jnp.int32, (K, 8, 128), 2) // 32
    last = got[0][:, 8:]
    for r in range(1, 4):
        last = jnp.where(block == r, pltpu.roll(got[r][:, 8:], 32 * r, 2), last)
    for j, v in enumerate(dense + [last]):
        g_buf[core, pl.ds(128 * j, 128), :] = v.reshape(128, 128).astype(BF16)
    g_copy = pltpu.make_async_remote_copy(
        src_ref=g_buf.at[core], dst_ref=g_buf.at[core], send_sem=g_ss, recv_sem=g_rs,
        device_id=sibling, device_id_type=MESH)
    g_copy.start()

    def place(half):
        v = g_buf[half].astype(F32).reshape(80, 8, 128)
        turn = pltpu.roll(v, 4, 1)
        sw = jnp.where(lax.broadcasted_iota(jnp.int32, (80, 8, 128), 1) < 4, -turn, turn)
        c_half, s_half = phase[0, half], phase[1, half]
        at = pl.multiple_of(128 * half, 128)
        m_ref[:, pl.ds(at, 128)] = (c_half * v + s_half * sw).reshape(LANES, 128).astype(BF16)
        m_ref[:, pl.ds(256 + at, 128)] = (c_half * sw - s_half * v).reshape(LANES, 128).astype(BF16)

    place(core)

    all_but_one(s_ss)
    all_but_one(m_ss)
    for g in range(len(GROUPS)):
        c_copy(g).wait_send()
    g_copy.wait_recv()
    place(1 - core)
    g_copy.wait_send()


def spectra(plume, weight, t8, t4, e):
    vmem = pl.BlockSpec(memory_space=pltpu.VMEM)
    anywhere = pl.BlockSpec(memory_space=pl.ANY)
    dma = pltpu.SemaphoreType.DMA
    return pl.pallas_call(
        spectra_kernel,
        out_shape=jax.ShapeDtypeStruct((LANES, 2 * K * K), BF16),
        in_specs=[anywhere] * 5,
        out_specs=vmem,
        scratch_shapes=[
            pltpu.VMEM((C, YL, ZL, NX), BF16),
            pltpu.VMEM((32, 2 * C * C), F32),
            pltpu.VMEM((256, NX), BF16),
            pltpu.VMEM((128, NX), BF16),
            pltpu.VMEM((CELLS, 512), BF16),
            pltpu.VMEM((256, 8 * NX), BF16),
            pltpu.VMEM((128, 4 * NX), BF16),
            pltpu.VMEM((256, CELLS), BF16),
            pltpu.VMEM((2, LANES, 128), BF16),
            pltpu.VMEM((LANES, 128), BF16),
            pltpu.VMEM((LANES, 128), F32),
            pltpu.VMEM((4, 16, 16, 128), BF16),
            pltpu.VMEM((64, 16, 128), BF16),
            pltpu.VMEM((40, 32), F32),
            pltpu.VMEM((2 * C * C, 32), F32),
            pltpu.VMEM((16, 128), BF16),
            pltpu.VMEM((4, 16, 16, 128), BF16),
            pltpu.VMEM((2, LANES, 128), BF16),
            pltpu.VMEM((2, 2, 8, 128), F32),
            dma((3,)), dma((3,)), dma,
            dma((3,)), dma((3,)),
            dma, dma((4,)),
            dma, dma,
            dma, dma,
        ],
        compiler_params=pltpu.CompilerParams(
            collective_id=0, has_side_effects=True, vmem_limit_bytes=56 * 2**20),
        name="spectra",
    )(plume, weight, t8, t4, e)


CHUNKS = 4


def output_kernel(plume, m_ref, e_ref, lw_ref, bias_ref, xi_ref, out, x_buf, o_buf, b_buf, kron, rhs, in_sem, out_sem):
    yt = YL // CHUNKS

    def load(i):
        rows = pl.ds(i * yt, yt)
        return pltpu.make_async_copy(plume.at[:, rows], x_buf.at[:, rows], in_sem.at[i])

    def store(i):
        rows = pl.ds(i * yt, yt)
        return pltpu.make_async_copy(o_buf.at[:, rows], out.at[:, rows], out_sem.at[i])

    for i in range(CHUNKS):
        load(i).start()
    spread = jnp.where(
        lax.broadcasted_iota(jnp.int32, (320, C), 0) // 16 == lax.broadcasted_iota(jnp.int32, (320, C), 1),
        F32(1.0), F32(0.0)).astype(BF16)
    rows20 = jnp.dot(spread, lw_ref[...], preferred_element_type=F32).astype(BF16)
    across = jnp.where(
        lax.broadcasted_iota(jnp.int32, (C, 384), 1) // 16 == lax.broadcasted_iota(jnp.int32, (C, 384), 0),
        F32(1.0), F32(0.0)).astype(BF16)
    full = jnp.dot(rows20, across, preferred_element_type=F32)
    row = lax.broadcasted_iota(jnp.int32, (320, 384), 0)
    col = lax.broadcasted_iota(jnp.int32, (320, 384), 1)
    full = jnp.where((row % 16) == (col % 16), full, F32(0.0))
    own = (lax.broadcasted_iota(jnp.int32, (320, C), 0) // 16 == lax.broadcasted_iota(jnp.int32, (320, C), 1))
    bias = jnp.sum(jnp.where(own, bias_ref[...], F32(0.0)), axis=1, keepdims=True)
    b1 = bias.astype(BF16).astype(F32)
    b2 = (bias - b1).astype(BF16).astype(F32)
    b3 = bias - b1 - b2
    full = jnp.where(col == 320, b1, full)
    full = jnp.where(col == 321, b2, full)
    full = jnp.where(col == 322, b3, full)
    kron[...] = full.astype(BF16)
    for s in range(2):
        rhs[s, pl.ds(0, 128), :] = xi_ref[...]
        rhs[s, pl.ds(192, 64), :] = jnp.where(
            lax.broadcasted_iota(jnp.int32, (64, NX), 0) < 16, F32(1.0), F32(0.0)).astype(BF16)
    lane = lax.broadcasted_iota(jnp.int32, (16, 128), 1) % 4
    masks = [lane == k for k in range(4)]

    def chunk(i, _):
        load(i).wait()
        cells = yt * ZL
        b_buf[...] = lax.dot_general(
            e_ref[pl.ds(pl.multiple_of(i * cells, cells), cells), :], m_ref[...], CONTRACT_LANES,
            preferred_element_type=F32).astype(BF16)
        for q in range(cells // 16):
            y, z, s = i * yt + q // 2, (q % 2) * 16, q % 2
            xs = x_buf[:, y, pl.ds(z, 16), :].reshape(320, NX)
            rhs[s, pl.ds(128, 64), :] = xs[256:]
            parts = []
            for o in range(C):
                v = b_buf[pl.ds(16 * q, 16), pl.ds(128 * (o // 4), 128)]
                parts.append(jnp.where(masks[o % 4], v, jnp.zeros_like(v)))
            left = jnp.concatenate([jnp.concatenate(parts, 0), kron[:, pl.ds(256, 128)]], 1)
            acc = jnp.dot(kron[:, pl.ds(0, 256)], xs[:256], preferred_element_type=F32)
            acc = acc + jnp.dot(left, rhs[s], preferred_element_type=F32)
            half = 0.5 * acc
            y_out = half + half * lax.erf(acc * F32(math.sqrt(0.5)))
            o_buf[:, y, pl.ds(z, 16), :] = y_out.astype(BF16).reshape(C, 16, NX)
        store(i).start()
        return 0

    lax.fori_loop(0, CHUNKS, chunk, 0)
    for i in range(CHUNKS):
        store(i).wait()


def output(plume, m, e, lw, bias, xi):
    vmem = pl.BlockSpec(memory_space=pltpu.VMEM)
    anywhere = pl.BlockSpec(memory_space=pl.ANY)
    dma = pltpu.SemaphoreType.DMA
    return pl.pallas_call(
        output_kernel,
        out_shape=jax.ShapeDtypeStruct((C, YL, ZL, NX), BF16),
        in_specs=[anywhere] + [vmem] * 5,
        out_specs=anywhere,
        scratch_shapes=[
            pltpu.VMEM((C, YL, ZL, NX), BF16),
            pltpu.VMEM((C, YL, ZL, NX), BF16),
            pltpu.VMEM((CELLS // CHUNKS, LANES), BF16),
            pltpu.VMEM((320, 384), BF16),
            pltpu.VMEM((2, 256, NX), BF16),
            dma((CHUNKS,)), dma((CHUNKS,)),
        ],
        compiler_params=pltpu.CompilerParams(vmem_limit_bytes=56 * 2**20),
        name="output",
    )(plume, m, e, lw, bias, xi)


def on_device(plume, weight, linear_weight, channel_bias):
    t8, t4 = forward_table()
    e = jnp.asarray(mode_table())
    m = spectra(plume, weight.reshape(32, 2 * C * C), jnp.asarray(t8), jnp.asarray(t4), e)
    return output(plume, m, e, linear_weight, channel_bias.reshape(1, C), jnp.asarray(inverse_table()))


def solution(mesh):
    return jax.shard_map(
        on_device, mesh=mesh,
        in_specs=(P(None, "wide", "narrow", None), P("wide", "narrow", None, None), P(), P()),
        out_specs=P(None, "wide", "narrow", None), check_vma=False)
```

time: 48.5 us -> 43.3 us (0.89)
  Pallas kernels: 46.9 us -> 43.2 us
  local copies, waits for them, and re-layouts: 1.5 us -> 0 us
    pallas_call x1, Pallas kernels: 34.6 us -> 30.5 us  [spectra(): pl.pallas_call(spectra_kernel, out_shape=jax.ShapeDtypeStruct((LANES, 2 *...]
    another operation x1 -> x0, local copies, waits for them, and re-layouts: 0.78 us -> none  [on_device(): bias = jnp.repeat(channel_bias, 16)[:, None]]
    broadcast_in_dim x1 -> x0, local copies, waits for them, and re-layouts: 0.72 us -> none  [on_device(): bias = jnp.repeat(channel_bias, 16)[:, None]]
where the time goes in v1:
time: 43.3 us; the launch traced here: 43.2 us
  Pallas kernels  43.2 us (100%)
    pallas_call x1, Pallas kernels, spectra(): pl.pallas_call(spectra_kernel, out_shape=jax.ShapeDtypeStruct((LANES, 2 *...  30.5 us
    pallas_call x1, Pallas kernels, output(): pl.pallas_call(output_kernel, out_shape=jax.ShapeDtypeStruct((C, YL, ZL,...  12.7 us

profile of v1, /device:TPU:1, one launch (start us, length us, event | category | flops | bytes accessed | tf_op | source)
XLA Modules:
  0.0 43.2 jit_solution(12849694001282970570)
XLA Ops:
  0.0 30.5 %spectra.1.m_ref = bf16[640,512]{1,0:T(8,128)(2,1)} custom-call(bf16[20,32,32,256]{3,2,1,0:T(8,128)(2,1)} %plume.3, f32[32,800]{1,0:T(8,128)} %bitcast.2, bf16[256,256]{1,0:T(8,128)(2,1)} %constant.9.clone.t8_hbm, bf16[128,256]{1,0:T(8,128)(2,1)} %constant.10.clone.t4_hbm, bf16[1024,512]{1,0:T(8,128)(2,1)} %constant.8.clone.e_ref), custom_call_target="tpu_custom_call" | custom-call | tf_op jit(solution)/shard_map/spectra/pallas_call | solution.py:298
  30.5 12.7 %output.1 = bf16[20,32,32,256]{3,2,1,0:T(8,128)(2,1)} custom-call(bf16[20,32,32,256]{3,2,1,0:T(8,128)(2,1)} %plume.3, bf16[640,512]{1,0:T(8,128)(2,1)} %spectra.1.m_ref, bf16[1024,512]{1,0:T(8,128)(2,1)} %constant.8.clone.e_ref, bf16[20,20]{1,0:T(8,128)(2,1)} %lw_ref.1, f32[1,20]{1,0:T(1,128)} %bitcast.3, bf16[128,256]{1,0:T(8,128)(2,1)} %constant.11.clone.xi_ref), custom_call_target="tpu_custom_call" | custom-call | tf_op jit(solution)/shard_map/output/pallas_call | solution.py:410

commit v2 on v1

--- a/solution.py
+++ b/solution.py
@@ -104,9 +104,9 @@
 
 
 def spectra_kernel(
-    plume, w_hbm, t8_hbm, t4_hbm, e_ref,
-    m_ref,
-    x_buf, w_ref, t8_ref, t4_ref, e_buf, tab8, tab4, a_buf, sib_send, sib_recv, mine, s_send, s_recv, q_buf, wt_buf, m_send, m_recv,
+    plume, w_hbm, t8_hbm, t4_hbm, e_ref, lw_hbm, bias_hbm, xi_hbm,
+    m_ref, x_buf, e_buf, kron, rhs,
+    w_ref, t8_ref, t4_ref, lw_ref, bias_ref, xi_ref, tab8, tab4, a_buf, sib_send, sib_recv, mine, s_send, s_recv, q_buf, wt_buf, m_send, m_recv,
     g_buf, phase,
     in_sem, w_sem, e_sem, c_ss, c_rs, s_ss, s_rs, m_ss, m_rs, g_ss, g_rs,
 ):
@@ -116,7 +116,8 @@
     sibling = (wide, narrow + 1 - 2 * core)
     e_copy = pltpu.make_async_copy(e_ref, e_buf, e_sem)
     small = [pltpu.make_async_copy(src, dst, w_sem.at[i]) for i, (src, dst) in enumerate(
-        ((t8_hbm, t8_ref), (t4_hbm, t4_ref), (w_hbm, w_ref)))]
+        ((t8_hbm, t8_ref), (t4_hbm, t4_ref), (w_hbm, w_ref), (lw_hbm, lw_ref), (bias_hbm, bias_ref),
+         (xi_hbm, xi_ref)))]
     for copy in small:
         copy.start()
     loads = []
@@ -143,7 +144,7 @@
     for _, dz, dy, dx in others:
         pl.semaphore_signal(barrier, inc=1, device_id=(wides[dy][dx], narrows[dz]), device_id_type=MESH)
 
-    for copy in small:
+    for copy in small[:2]:
         copy.wait()
     r8 = lax.broadcasted_iota(jnp.int32, (256, NX), 0) % 8
     r4 = lax.broadcasted_iota(jnp.int32, (128, NX), 0) % 4
@@ -157,9 +158,6 @@
         phase[1, h] = sin_v[:, 128 * h:128 * h + 128]
     scale = F32(1.0 / math.sqrt(NX * NY * NZ))
     pc, ps = cos_v * scale, sin_v * scale
-    for k in range(7):
-        width = min(128, 2 * C * C - 128 * k)
-        wt_buf[pl.ds(128 * k, width), :] = w_ref[:, pl.ds(128 * k, width)].T
 
     def c_copy(g):
         c0, nc, row0 = GROUPS[g]
@@ -223,131 +221,11 @@
         ref = buf.at[pl.ds(max(1, 16 * part), 16 if part else 15)]
         pltpu.make_async_copy(ref, ref, sems.at[part]).wait()
 
-    total = s_send[z, wide].astype(F32)
-    for part in (0, 1, 3, 2):
-        first = max(1, 16 * part)
-        arrived(s_recv, s_rs, part)
-        total = total + jnp.sum(s_recv[pl.ds(first, 16 * part + 16 - first)].astype(F32), axis=0)
-    for t in range(4):
-        v = total[0:8] if t == 0 else pltpu.roll(total[0:8], 128 - 32 * t, 1)
-        q_buf[pl.ds(8 * t, 8), :] = v[:, :32]
-    q_buf[pl.ds(32, 8), :] = total[8:16, :32]
-
-    out_re = jnp.zeros((C, 32), F32)
-    out_im = jnp.zeros((C, 32), F32)
-    for c in range(C):
-        s_re = q_buf[pl.ds(row_of(0, c), 1), :]
-        s_im = q_buf[pl.ds(row_of(1, c), 1), :]
-        w_re = wt_buf[pl.ds(C * c, C), :]
-        w_im = wt_buf[pl.ds(C * C + C * c, C), :]
-        out_re = out_re + (w_re * s_re - w_im * s_im)
-        out_im = out_im + (w_re * s_im + w_im * s_re)
-    tiles = [jnp.concatenate([out_re[4 * j:4 * j + 4], out_im[4 * j:4 * j + 4]], axis=0) for j in range(5)]
-    m_send[...] = jnp.concatenate(
-        [jnp.concatenate(tiles[:4], axis=1),
-         jnp.concatenate([tiles[4], jnp.zeros((8, 96), F32)], axis=1)], axis=0).astype(BF16)
-
-    for slot, dz, dy, dx in others:
-        pltpu.make_async_remote_copy(
-            src_ref=m_send, dst_ref=m_recv.at[z, wide], send_sem=m_ss, recv_sem=m_rs,
-            device_id=(wides[dy][dx], narrows[dz]), device_id_type=MESH).start()
-    m_recv[z, wide] = m_send[...]
-
-    def all_but_one(sem):
-        ref = s_recv.at[pl.ds(1, 63)]
-        pltpu.make_async_copy(ref, ref, sem).wait()
-
-    all_but_one(m_rs)
-    got = [m_recv[r].astype(F32) for r in range(4)]
-    dense = block_turn([v[:, :8] for v in got])
-    block = lax.broadcasted_iota(jnp.int32, (K, 8, 128), 2) // 32
-    last = got[0][:, 8:]
-    for r in range(1, 4):
-        last = jnp.where(block == r, pltpu.roll(got[r][:, 8:], 32 * r, 2), last)
-    for j, v in enumerate(dense + [last]):
-        g_buf[core, pl.ds(128 * j, 128), :] = v.reshape(128, 128).astype(BF16)
-    g_copy = pltpu.make_async_remote_copy(
-        src_ref=g_buf.at[core], dst_ref=g_buf.at[core], send_sem=g_ss, recv_sem=g_rs,
-        device_id=sibling, device_id_type=MESH)
-    g_copy.start()
-
-    def place(half):
-        v = g_buf[half].astype(F32).reshape(80, 8, 128)
-        turn = pltpu.roll(v, 4, 1)
-        sw = jnp.where(lax.broadcasted_iota(jnp.int32, (80, 8, 128), 1) < 4, -turn, turn)
-        c_half, s_half = phase[0, half], phase[1, half]
-        at = pl.multiple_of(128 * half, 128)
-        m_ref[:, pl.ds(at, 128)] = (c_half * v + s_half * sw).reshape(LANES, 128).astype(BF16)
-        m_ref[:, pl.ds(256 + at, 128)] = (c_half * sw - s_half * v).reshape(LANES, 128).astype(BF16)
-
-    place(core)
-
-    all_but_one(s_ss)
-    all_but_one(m_ss)
-    for g in range(len(GROUPS)):
-        c_copy(g).wait_send()
-    g_copy.wait_recv()
-    place(1 - core)
-    g_copy.wait_send()
-
-
-def spectra(plume, weight, t8, t4, e):
-    vmem = pl.BlockSpec(memory_space=pltpu.VMEM)
-    anywhere = pl.BlockSpec(memory_space=pl.ANY)
-    dma = pltpu.SemaphoreType.DMA
-    return pl.pallas_call(
-        spectra_kernel,
-        out_shape=jax.ShapeDtypeStruct((LANES, 2 * K * K), BF16),
-        in_specs=[anywhere] * 5,
-        out_specs=vmem,
-        scratch_shapes=[
-            pltpu.VMEM((C, YL, ZL, NX), BF16),
-            pltpu.VMEM((32, 2 * C * C), F32),
-            pltpu.VMEM((256, NX), BF16),
-            pltpu.VMEM((128, NX), BF16),
-            pltpu.VMEM((CELLS, 512), BF16),
-            pltpu.VMEM((256, 8 * NX), BF16),
-            pltpu.VMEM((128, 4 * NX), BF16),
-            pltpu.VMEM((256, CELLS), BF16),
-            pltpu.VMEM((2, LANES, 128), BF16),
-            pltpu.VMEM((LANES, 128), BF16),
-            pltpu.VMEM((LANES, 128), F32),
-            pltpu.VMEM((4, 16, 16, 128), BF16),
-            pltpu.VMEM((64, 16, 128), BF16),
-            pltpu.VMEM((40, 32), F32),
-            pltpu.VMEM((2 * C * C, 32), F32),
-            pltpu.VMEM((16, 128), BF16),
-            pltpu.VMEM((4, 16, 16, 128), BF16),
-            pltpu.VMEM((2, LANES, 128), BF16),
-            pltpu.VMEM((2, 2, 8, 128), F32),
-            dma((3,)), dma((3,)), dma,
-            dma((3,)), dma((3,)),
-            dma, dma((4,)),
-            dma, dma,
-            dma, dma,
-        ],
-        compiler_params=pltpu.CompilerParams(
-            collective_id=0, has_side_effects=True, vmem_limit_bytes=56 * 2**20),
-        name="spectra",
-    )(plume, weight, t8, t4, e)
-
-
-CHUNKS = 4
-
-
-def output_kernel(plume, m_ref, e_ref, lw_ref, bias_ref, xi_ref, out, x_buf, o_buf, b_buf, kron, rhs, in_sem, out_sem):
-    yt = YL // CHUNKS
-
-    def load(i):
-        rows = pl.ds(i * yt, yt)
-        return pltpu.make_async_copy(plume.at[:, rows], x_buf.at[:, rows], in_sem.at[i])
-
-    def store(i):
-        rows = pl.ds(i * yt, yt)
-        return pltpu.make_async_copy(o_buf.at[:, rows], out.at[:, rows], out_sem.at[i])
-
-    for i in range(CHUNKS):
-        load(i).start()
+    for copy in small[2:]:
+        copy.wait()
+    for k in range(7):
+        width = min(128, 2 * C * C - 128 * k)
+        wt_buf[pl.ds(128 * k, width), :] = w_ref[:, pl.ds(128 * k, width)].T
     spread = jnp.where(
         lax.broadcasted_iota(jnp.int32, (320, C), 0) // 16 == lax.broadcasted_iota(jnp.int32, (320, C), 1),
         F32(1.0), F32(0.0)).astype(BF16)
@@ -372,11 +250,136 @@
         rhs[s, pl.ds(0, 128), :] = xi_ref[...]
         rhs[s, pl.ds(192, 64), :] = jnp.where(
             lax.broadcasted_iota(jnp.int32, (64, NX), 0) < 16, F32(1.0), F32(0.0)).astype(BF16)
+    total = s_send[z, wide].astype(F32)
+    for part in (0, 1, 3, 2):
+        first = max(1, 16 * part)
+        arrived(s_recv, s_rs, part)
+        total = total + jnp.sum(s_recv[pl.ds(first, 16 * part + 16 - first)].astype(F32), axis=0)
+    for t in range(4):
+        v = total[0:8] if t == 0 else pltpu.roll(total[0:8], 128 - 32 * t, 1)
+        q_buf[pl.ds(8 * t, 8), :] = v[:, :32]
+    q_buf[pl.ds(32, 8), :] = total[8:16, :32]
+
+    out_re = jnp.zeros((C, 32), F32)
+    out_im = jnp.zeros((C, 32), F32)
+    for c in range(C):
+        s_re = q_buf[pl.ds(row_of(0, c), 1), :]
+        s_im = q_buf[pl.ds(row_of(1, c), 1), :]
+        w_re = wt_buf[pl.ds(C * c, C), :]
+        w_im = wt_buf[pl.ds(C * C + C * c, C), :]
+        out_re = out_re + (w_re * s_re - w_im * s_im)
+        out_im = out_im + (w_re * s_im + w_im * s_re)
+    tiles = [jnp.concatenate([out_re[4 * j:4 * j + 4], out_im[4 * j:4 * j + 4]], axis=0) for j in range(5)]
+    m_send[...] = jnp.concatenate(
+        [jnp.concatenate(tiles[:4], axis=1),
+         jnp.concatenate([tiles[4], jnp.zeros((8, 96), F32)], axis=1)], axis=0).astype(BF16)
+
+    for slot, dz, dy, dx in others:
+        pltpu.make_async_remote_copy(
+            src_ref=m_send, dst_ref=m_recv.at[z, wide], send_sem=m_ss, recv_sem=m_rs,
+            device_id=(wides[dy][dx], narrows[dz]), device_id_type=MESH).start()
+    m_recv[z, wide] = m_send[...]
+
+    def all_but_one(sem):
+        ref = s_recv.at[pl.ds(1, 63)]
+        pltpu.make_async_copy(ref, ref, sem).wait()
+
+    all_but_one(m_rs)
+    got = [m_recv[r].astype(F32) for r in range(4)]
+    dense = block_turn([v[:, :8] for v in got])
+    block = lax.broadcasted_iota(jnp.int32, (K, 8, 128), 2) // 32
+    last = got[0][:, 8:]
+    for r in range(1, 4):
+        last = jnp.where(block == r, pltpu.roll(got[r][:, 8:], 32 * r, 2), last)
+    for j, v in enumerate(dense + [last]):
+        g_buf[core, pl.ds(128 * j, 128), :] = v.reshape(128, 128).astype(BF16)
+    g_copy = pltpu.make_async_remote_copy(
+        src_ref=g_buf.at[core], dst_ref=g_buf.at[core], send_sem=g_ss, recv_sem=g_rs,
+        device_id=sibling, device_id_type=MESH)
+    g_copy.start()
+
+    def place(half):
+        v = g_buf[half].astype(F32).reshape(80, 8, 128)
+        turn = pltpu.roll(v, 4, 1)
+        sw = jnp.where(lax.broadcasted_iota(jnp.int32, (80, 8, 128), 1) < 4, -turn, turn)
+        c_half, s_half = phase[0, half], phase[1, half]
+        at = pl.multiple_of(128 * half, 128)
+        m_ref[:, pl.ds(at, 128)] = (c_half * v + s_half * sw).reshape(LANES, 128).astype(BF16)
+        m_ref[:, pl.ds(256 + at, 128)] = (c_half * sw - s_half * v).reshape(LANES, 128).astype(BF16)
+
+    place(core)
+
+    all_but_one(s_ss)
+    all_but_one(m_ss)
+    for g in range(len(GROUPS)):
+        c_copy(g).wait_send()
+    g_copy.wait_recv()
+    place(1 - core)
+    g_copy.wait_send()
+
+
+def spectra(plume, weight, t8, t4, e, lw, bias, xi):
+    vmem = pl.BlockSpec(memory_space=pltpu.VMEM)
+    anywhere = pl.BlockSpec(memory_space=pl.ANY)
+    dma = pltpu.SemaphoreType.DMA
+    return pl.pallas_call(
+        spectra_kernel,
+        out_shape=(
+            pltpu.VMEM((LANES, 2 * K * K), BF16),
+            pltpu.VMEM((C, YL, ZL, NX), BF16),
+            pltpu.VMEM((CELLS, 512), BF16),
+            pltpu.VMEM((320, 384), BF16),
+            pltpu.VMEM((2, 256, NX), BF16),
+        ),
+        in_specs=[anywhere] * 8,
+        out_specs=(vmem,) * 5,
+        scratch_shapes=[
+            pltpu.VMEM((32, 2 * C * C), F32),
+            pltpu.VMEM((256, NX), BF16),
+            pltpu.VMEM((128, NX), BF16),
+            pltpu.VMEM((C, C), BF16),
+            pltpu.VMEM((1, C), F32),
+            pltpu.VMEM((128, NX), BF16),
+            pltpu.VMEM((256, 8 * NX), BF16),
+            pltpu.VMEM((128, 4 * NX), BF16),
+            pltpu.VMEM((256, CELLS), BF16),
+            pltpu.VMEM((2, LANES, 128), BF16),
+            pltpu.VMEM((LANES, 128), BF16),
+            pltpu.VMEM((LANES, 128), F32),
+            pltpu.VMEM((4, 16, 16, 128), BF16),
+            pltpu.VMEM((64, 16, 128), BF16),
+            pltpu.VMEM((40, 32), F32),
+            pltpu.VMEM((2 * C * C, 32), F32),
+            pltpu.VMEM((16, 128), BF16),
+            pltpu.VMEM((4, 16, 16, 128), BF16),
+            pltpu.VMEM((2, LANES, 128), BF16),
+            pltpu.VMEM((2, 2, 8, 128), F32),
+            dma((3,)), dma((6,)), dma,
+            dma((3,)), dma((3,)),
+            dma, dma((4,)),
+            dma, dma,
+            dma, dma,
+        ],
+        compiler_params=pltpu.CompilerParams(
+            collective_id=0, has_side_effects=True, vmem_limit_bytes=51 * 2**20),
+        name="spectra",
+    )(plume, weight, t8, t4, e, lw, bias, xi)
+
+
+CHUNKS = 4
+
+
+def output_kernel(m_ref, x_buf, e_ref, kron, rhs, out, o_buf, b_buf, out_sem):
+    yt = YL // CHUNKS
+
+    def store(i):
+        rows = pl.ds(i * yt, yt)
+        return pltpu.make_async_copy(o_buf.at[:, rows], out.at[:, rows], out_sem.at[i])
+
     lane = lax.broadcasted_iota(jnp.int32, (16, 128), 1) % 4
     masks = [lane == k for k in range(4)]
 
     def chunk(i, _):
-        load(i).wait()
         cells = yt * ZL
         b_buf[...] = lax.dot_general(
             e_ref[pl.ds(pl.multiple_of(i * cells, cells), cells), :], m_ref[...], CONTRACT_LANES,
@@ -403,33 +406,28 @@
         store(i).wait()
 
 
-def output(plume, m, e, lw, bias, xi):
+def output(m, x, e, kron, rhs):
     vmem = pl.BlockSpec(memory_space=pltpu.VMEM)
-    anywhere = pl.BlockSpec(memory_space=pl.ANY)
-    dma = pltpu.SemaphoreType.DMA
     return pl.pallas_call(
         output_kernel,
         out_shape=jax.ShapeDtypeStruct((C, YL, ZL, NX), BF16),
-        in_specs=[anywhere] + [vmem] * 5,
-        out_specs=anywhere,
+        in_specs=[vmem] * 5,
+        out_specs=pl.BlockSpec(memory_space=pltpu.HBM),
         scratch_shapes=[
             pltpu.VMEM((C, YL, ZL, NX), BF16),
-            pltpu.VMEM((C, YL, ZL, NX), BF16),
             pltpu.VMEM((CELLS // CHUNKS, LANES), BF16),
-            pltpu.VMEM((320, 384), BF16),
-            pltpu.VMEM((2, 256, NX), BF16),
-            dma((CHUNKS,)), dma((CHUNKS,)),
+            pltpu.SemaphoreType.DMA((CHUNKS,)),
         ],
-        compiler_params=pltpu.CompilerParams(vmem_limit_bytes=56 * 2**20),
+        compiler_params=pltpu.CompilerParams(vmem_limit_bytes=16 * 2**20),
         name="output",
-    )(plume, m, e, lw, bias, xi)
+    )(m, x, e, kron, rhs)
 
 
 def on_device(plume, weight, linear_weight, channel_bias):
     t8, t4 = forward_table()
-    e = jnp.asarray(mode_table())
-    m = spectra(plume, weight.reshape(32, 2 * C * C), jnp.asarray(t8), jnp.asarray(t4), e)
-    return output(plume, m, e, linear_weight, channel_bias.reshape(1, C), jnp.asarray(inverse_table()))
+    return output(*spectra(
+        plume, weight.reshape(32, 2 * C * C), jnp.asarray(t8), jnp.asarray(t4), jnp.asarray(mode_table()),
+        linear_weight, channel_bias.reshape(1, C), jnp.asarray(inverse_table())))
 
 
 def solution(mesh):

time: 43.3 us -> 38.6 us (0.89)
  Pallas kernels: 43.2 us -> 38.5 us
    pallas_call x1, Pallas kernels: 12.7 us -> 9.25 us  [output(): pl.pallas_call(output_kernel, out_shape=jax.ShapeDtypeStruct((C, YL, ZL,...]
    pallas_call x1, Pallas kernels: 30.5 us -> 29.2 us  [spectra(): pl.pallas_call(spectra_kernel, out_shape=(pltpu.VMEM((LANES, 2 * K * K),...]
where the time goes in v2:
time: 38.6 us; the launch traced here: 38.5 us
  Pallas kernels  38.5 us (100%)
    pallas_call x1, Pallas kernels, spectra(): pl.pallas_call(spectra_kernel, out_shape=(pltpu.VMEM((LANES, 2 * K * K),...  29.2 us
    pallas_call x1, Pallas kernels, output(): pl.pallas_call(output_kernel, out_shape=jax.ShapeDtypeStruct((C, YL, ZL,...  9.25 us

profile of v2, /device:TPU:1, one launch (start us, length us, event | category | flops | bytes accessed | tf_op | source)
XLA Modules:
  0.0 38.5 jit_solution(10980853122276670043)
XLA Ops:
  0.0 29.2 %spectra.1 = (bf16[640,512]{1,0:T(8,128)(2,1)S(1)}, bf16[20,32,32,256]{3,2,1,0:T(8,128)(2,1)S(1)}, bf16[1024,512]{1,0:T(8,128)(2,1)S(1)}, bf16[320,384]{1,0:T(8,128)(2,1)S(1)}, bf16[2,256,256]{2,1,0:T(8,128)(2,1)S(1)}) custom-call(bf16[20,32,32,256]{3,2,1,0:T(8,128)(2,1)} %plume.1, f32[32,800]{1,0:T(8,128)} %bitcast.2, ...), custom_call_target="tpu_custom_call" | custom-call | tf_op jit(solution)/shard_map/spectra/pallas_call | solution.py:325
  29.3 9.2 %output.1 = bf16[20,32,32,256]{3,2,1,0:T(8,128)(2,1)} custom-call(bf16[640,512]{1,0:T(8,128)(2,1)S(1)} %get-tuple-element.10.m_ref, bf16[20,32,32,256]{3,2,1,0:T(8,128)(2,1)S(1)} %get-tuple-element.11.x_buf, bf16[1024,512]{1,0:T(8,128)(2,1)S(1)} %get-tuple-element.12.e_ref, bf16[320,384]{1,0:T(8,128)(2,1)S(1)} %get-tuple-element.13.kron, ...), custom_call_target="tpu_custom_call" | custom-call | tf_op jit(solution)/shard_map/output/pallas_call | solution.py:411

commit v3 on v2

--- a/solution.py
+++ b/solution.py
@@ -118,7 +118,7 @@
     small = [pltpu.make_async_copy(src, dst, w_sem.at[i]) for i, (src, dst) in enumerate(
         ((t8_hbm, t8_ref), (t4_hbm, t4_ref), (w_hbm, w_ref), (lw_hbm, lw_ref), (bias_hbm, bias_ref),
          (xi_hbm, xi_ref)))]
-    for copy in small:
+    for copy in small[:2]:
         copy.start()
     loads = []
     for g, (c0, nc, _) in enumerate(GROUPS):
@@ -127,6 +127,8 @@
         loads.append(copy)
         if g == 0:
             e_copy.start()
+    for copy in small[2:]:
+        copy.start()
 
     rows_of_chips = [4 * lax.rem(y + d, 4) for d in range(4)]
     places = [lax.rem(x + d, 4) for d in range(4)]
@@ -291,12 +293,15 @@
     last = got[0][:, 8:]
     for r in range(1, 4):
         last = jnp.where(block == r, pltpu.roll(got[r][:, 8:], 32 * r, 2), last)
+    def g_copy(j):
+        rows = pl.ds(128 * j, 128)
+        return pltpu.make_async_remote_copy(
+            src_ref=g_buf.at[core, rows], dst_ref=g_buf.at[core, rows], send_sem=g_ss.at[j], recv_sem=g_rs.at[j],
+            device_id=sibling, device_id_type=MESH)
+
     for j, v in enumerate(dense + [last]):
         g_buf[core, pl.ds(128 * j, 128), :] = v.reshape(128, 128).astype(BF16)
-    g_copy = pltpu.make_async_remote_copy(
-        src_ref=g_buf.at[core], dst_ref=g_buf.at[core], send_sem=g_ss, recv_sem=g_rs,
-        device_id=sibling, device_id_type=MESH)
-    g_copy.start()
+        g_copy(j).start()
 
     def place(half):
         v = g_buf[half].astype(F32).reshape(80, 8, 128)
@@ -313,9 +318,11 @@
     all_but_one(m_ss)
     for g in range(len(GROUPS)):
         c_copy(g).wait_send()
-    g_copy.wait_recv()
+    for j in range(5):
+        g_copy(j).wait_recv()
     place(1 - core)
-    g_copy.wait_send()
+    for j in range(5):
+        g_copy(j).wait_send()
 
 
 def spectra(plume, weight, t8, t4, e, lw, bias, xi):
@@ -358,7 +365,7 @@
             dma((3,)), dma((3,)),
             dma, dma((4,)),
             dma, dma,
-            dma, dma,
+            dma((5,)), dma((5,)),
         ],
         compiler_params=pltpu.CompilerParams(
             collective_id=0, has_side_effects=True, vmem_limit_bytes=51 * 2**20),
@@ -367,13 +374,14 @@
 
 
 CHUNKS = 4
+STORED = 2
 
 
 def output_kernel(m_ref, x_buf, e_ref, kron, rhs, out, o_buf, b_buf, out_sem):
     yt = YL // CHUNKS
 
     def store(i):
-        rows = pl.ds(i * yt, yt)
+        rows = pl.ds(i * STORED, STORED)
         return pltpu.make_async_copy(o_buf.at[:, rows], out.at[:, rows], out_sem.at[i])
 
     lane = lax.broadcasted_iota(jnp.int32, (16, 128), 1) % 4
@@ -387,22 +395,24 @@
         for q in range(cells // 16):
             y, z, s = i * yt + q // 2, (q % 2) * 16, q % 2
             xs = x_buf[:, y, pl.ds(z, 16), :].reshape(320, NX)
-            rhs[s, pl.ds(128, 64), :] = xs[256:]
             parts = []
             for o in range(C):
                 v = b_buf[pl.ds(16 * q, 16), pl.ds(128 * (o // 4), 128)]
                 parts.append(jnp.where(masks[o % 4], v, jnp.zeros_like(v)))
             left = jnp.concatenate([jnp.concatenate(parts, 0), kron[:, pl.ds(256, 128)]], 1)
-            acc = jnp.dot(kron[:, pl.ds(0, 256)], xs[:256], preferred_element_type=F32)
-            acc = acc + jnp.dot(left, rhs[s], preferred_element_type=F32)
+            left = jnp.concatenate([kron[:, pl.ds(0, 256)], left], 1)
+            right = jnp.concatenate(
+                [xs[:256], rhs[0, pl.ds(0, 128), :], xs[256:], rhs[0, pl.ds(192, 64), :]], 0)
+            acc = jnp.dot(left, right, preferred_element_type=F32)
             half = 0.5 * acc
             y_out = half + half * lax.erf(acc * F32(math.sqrt(0.5)))
             o_buf[:, y, pl.ds(z, 16), :] = y_out.astype(BF16).reshape(C, 16, NX)
-        store(i).start()
+            if q % (2 * STORED) == 2 * STORED - 1:
+                store(i * (yt // STORED) + q // (2 * STORED)).start()
         return 0
 
     lax.fori_loop(0, CHUNKS, chunk, 0)
-    for i in range(CHUNKS):
+    for i in range(YL // STORED):
         store(i).wait()
 
 
@@ -416,7 +426,7 @@
         scratch_shapes=[
             pltpu.VMEM((C, YL, ZL, NX), BF16),
             pltpu.VMEM((CELLS // CHUNKS, LANES), BF16),
-            pltpu.SemaphoreType.DMA((CHUNKS,)),
+            pltpu.SemaphoreType.DMA((YL // STORED,)),
         ],
         compiler_params=pltpu.CompilerParams(vmem_limit_bytes=16 * 2**20),
         name="output",

time: 38.6 us -> 37.8 us (0.979)
  Pallas kernels: 38.5 us -> 37.6 us
    pallas_call x1, Pallas kernels: 9.25 us -> 8.43 us  [output(): pl.pallas_call(output_kernel, out_shape=jax.ShapeDtypeStruct((C, YL, ZL,...]
where the time goes in v3:
time: 37.8 us; the launch traced here: 37.7 us
  Pallas kernels  37.6 us (99%)
    pallas_call x1, Pallas kernels, spectra(): pl.pallas_call(spectra_kernel, out_shape=(pltpu.VMEM((LANES, 2 * K * K),...  29.2 us
    pallas_call x1, Pallas kernels, output(): pl.pallas_call(output_kernel, out_shape=jax.ShapeDtypeStruct((C, YL, ZL,...  8.43 us

profile of v3, /device:TPU:1, one launch (start us, length us, event | category | flops | bytes accessed | tf_op | source)
XLA Modules:
  0.0 37.7 jit_solution(2887439229053652260)
XLA Ops:
  0.0 29.2 %spectra.1 = (bf16[640,512]{1,0:T(8,128)(2,1)S(1)}, bf16[20,32,32,256]{3,2,1,0:T(8,128)(2,1)S(1)}, bf16[1024,512]{1,0:T(8,128)(2,1)S(1)}, bf16[320,384]{1,0:T(8,128)(2,1)S(1)}, bf16[2,256,256]{2,1,0:T(8,128)(2,1)S(1)}) custom-call(bf16[20,32,32,256]{3,2,1,0:T(8,128)(2,1)} %plume.1, f32[32,800]{1,0:T(8,128)} %bitcast.2, ...), custom_call_target="tpu_custom_call" | custom-call | tf_op jit(solution)/shard_map/spectra/pallas_call | solution.py:332
  29.2 8.4 %output.1 = bf16[20,32,32,256]{3,2,1,0:T(8,128)(2,1)} custom-call(bf16[640,512]{1,0:T(8,128)(2,1)S(1)} %get-tuple-element.10.m_ref, bf16[20,32,32,256]{3,2,1,0:T(8,128)(2,1)S(1)} %get-tuple-element.11.x_buf, bf16[1024,512]{1,0:T(8,128)(2,1)S(1)} %get-tuple-element.12.e_ref, bf16[320,384]{1,0:T(8,128)(2,1)S(1)} %get-tuple-element.13.kron, ...), custom_call_target="tpu_custom_call" | custom-call | tf_op jit(solution)/shard_map/output/pallas_call | solution.py:421

commit v4 on v3

--- a/solution.py
+++ b/solution.py
@@ -138,7 +138,7 @@
     far = (0, 1, 2, 1)
     others = sorted(
         [(16 * dz + 4 * dy + dx, dz, dy, dx) for dz in range(4) for dy in range(4) for dx in range(4)][1:],
-        key=lambda v: (-(far[v[1]] + far[v[2]] + far[v[3]]), v))
+        key=lambda v: (-(far[v[1]] + far[v[2]] + far[v[3]]), (v[0] * 37) % 64))
 
     barrier = pltpu.get_barrier_semaphore()
     pl.semaphore_signal(barrier, inc=1, device_id=sibling, device_id_type=MESH)
@@ -373,7 +373,7 @@
     )(plume, weight, t8, t4, e, lw, bias, xi)
 
 
-CHUNKS = 4
+CHUNKS = 2
 STORED = 2
 
 
@@ -403,10 +403,11 @@
             left = jnp.concatenate([kron[:, pl.ds(0, 256)], left], 1)
             right = jnp.concatenate(
                 [xs[:256], rhs[0, pl.ds(0, 128), :], xs[256:], rhs[0, pl.ds(192, 64), :]], 0)
-            acc = jnp.dot(left, right, preferred_element_type=F32)
-            half = 0.5 * acc
-            y_out = half + half * lax.erf(acc * F32(math.sqrt(0.5)))
-            o_buf[:, y, pl.ds(z, 16), :] = y_out.astype(BF16).reshape(C, 16, NX)
+            for h in range(2):
+                acc = jnp.dot(left[160 * h:160 * h + 160], right, preferred_element_type=F32)
+                half = 0.5 * acc
+                y_out = half + half * lax.erf(acc * F32(math.sqrt(0.5)))
+                o_buf[pl.ds(10 * h, 10), y, pl.ds(z, 16), :] = y_out.astype(BF16).reshape(10, 16, NX)
             if q % (2 * STORED) == 2 * STORED - 1:
                 store(i * (yt // STORED) + q // (2 * STORED)).start()
         return 0

time: 37.8 us -> 37.4 us (0.989)
  no operation moved by 1% of the time
where the time goes in v4:
time: 37.4 us; the launch traced here: 37.3 us
  Pallas kernels  37.3 us (100%)
    pallas_call x1, Pallas kernels, spectra(): pl.pallas_call(spectra_kernel, out_shape=(pltpu.VMEM((LANES, 2 * K * K),...  29 us
    pallas_call x1, Pallas kernels, output(): pl.pallas_call(output_kernel, out_shape=jax.ShapeDtypeStruct((C, YL, ZL,...  8.32 us

profile of v4, /device:TPU:1, one launch (start us, length us, event | category | flops | bytes accessed | tf_op | source)
XLA Modules:
  0.0 37.3 jit_solution(10536271045393547287)
XLA Ops:
  0.0 29.0 %spectra.1 = (bf16[640,512]{1,0:T(8,128)(2,1)S(1)}, bf16[20,32,32,256]{3,2,1,0:T(8,128)(2,1)S(1)}, bf16[1024,512]{1,0:T(8,128)(2,1)S(1)}, bf16[320,384]{1,0:T(8,128)(2,1)S(1)}, bf16[2,256,256]{2,1,0:T(8,128)(2,1)S(1)}) custom-call(bf16[20,32,32,256]{3,2,1,0:T(8,128)(2,1)} %plume.1, f32[32,800]{1,0:T(8,128)} %bitcast.2, ...), custom_call_target="tpu_custom_call" | custom-call | tf_op jit(solution)/shard_map/spectra/pallas_call | solution.py:332
  29.0 8.3 %output.1 = bf16[20,32,32,256]{3,2,1,0:T(8,128)(2,1)} custom-call(bf16[640,512]{1,0:T(8,128)(2,1)S(1)} %get-tuple-element.10.m_ref, bf16[20,32,32,256]{3,2,1,0:T(8,128)(2,1)S(1)} %get-tuple-element.11.x_buf, bf16[1024,512]{1,0:T(8,128)(2,1)S(1)} %get-tuple-element.12.e_ref, bf16[320,384]{1,0:T(8,128)(2,1)S(1)} %get-tuple-element.13.kron, ...), custom_call_target="tpu_custom_call" | custom-call | tf_op jit(solution)/shard_map/output/pallas_call | solution.py:422

commit v5 on v4

--- a/solution.py
+++ b/solution.py
@@ -138,7 +138,7 @@
     far = (0, 1, 2, 1)
     others = sorted(
         [(16 * dz + 4 * dy + dx, dz, dy, dx) for dz in range(4) for dy in range(4) for dx in range(4)][1:],
-        key=lambda v: (-(far[v[1]] + far[v[2]] + far[v[3]]), (v[0] * 37) % 64))
+        key=lambda v: (-(far[v[1]] + far[v[2]] + far[v[3]]), (v[0] * 21) % 64))
 
     barrier = pltpu.get_barrier_semaphore()
     pl.semaphore_signal(barrier, inc=1, device_id=sibling, device_id_type=MESH)
@@ -374,7 +374,7 @@
 
 
 CHUNKS = 2
-STORED = 2
+STORED = 1
 
 
 def output_kernel(m_ref, x_buf, e_ref, kron, rhs, out, o_buf, b_buf, out_sem):

time: 37.4 us -> 38.2 us (1.021)
  Pallas kernels: 37.3 us -> 38.1 us
    pallas_call x1, Pallas kernels: 29 us -> 29.5 us  [spectra(): pl.pallas_call(spectra_kernel, out_shape=(pltpu.VMEM((LANES, 2 * K * K),...]
where the time goes in v5:
time: 38.2 us; the launch traced here: 38.1 us
  Pallas kernels  38.1 us (100%)
    pallas_call x1, Pallas kernels, spectra(): pl.pallas_call(spectra_kernel, out_shape=(pltpu.VMEM((LANES, 2 * K * K),...  29.5 us
    pallas_call x1, Pallas kernels, output(): pl.pallas_call(output_kernel, out_shape=jax.ShapeDtypeStruct((C, YL, ZL,...  8.62 us

profile of v5, /device:TPU:1, one launch (start us, length us, event | category | flops | bytes accessed | tf_op | source)
XLA Modules:
  0.0 38.1 jit_solution(10729388849738412944)
XLA Ops:
  0.0 29.5 %spectra.1 = (bf16[640,512]{1,0:T(8,128)(2,1)S(1)}, bf16[20,32,32,256]{3,2,1,0:T(8,128)(2,1)S(1)}, bf16[1024,512]{1,0:T(8,128)(2,1)S(1)}, bf16[320,384]{1,0:T(8,128)(2,1)S(1)}, bf16[2,256,256]{2,1,0:T(8,128)(2,1)S(1)}) custom-call(bf16[20,32,32,256]{3,2,1,0:T(8,128)(2,1)} %plume.1, f32[32,800]{1,0:T(8,128)} %bitcast.2, ...), custom_call_target="tpu_custom_call" | custom-call | tf_op jit(solution)/shard_map/spectra/pallas_call | solution.py:332
  29.5 8.6 %output.1 = bf16[20,32,32,256]{3,2,1,0:T(8,128)(2,1)} custom-call(bf16[640,512]{1,0:T(8,128)(2,1)S(1)} %get-tuple-element.10.m_ref, bf16[20,32,32,256]{3,2,1,0:T(8,128)(2,1)S(1)} %get-tuple-element.11.x_buf, bf16[1024,512]{1,0:T(8,128)(2,1)S(1)} %get-tuple-element.12.e_ref, bf16[320,384]{1,0:T(8,128)(2,1)S(1)} %get-tuple-element.13.kron, ...), custom_call_target="tpu_custom_call" | custom-call | tf_op jit(solution)/shard_map/output/pallas_call | solution.py:422
